TPU v7x, 32 devices: a whole 2x2x4 slice. The times are simulated.
32 devices in a mesh: sector: 8 (over z, y), mpo: 4 (over x, core).
Axes of the slice: x: 2, y: 2, z: 4, core: 2. Of those that a mesh axis runs over, the one named last changes fastest.
Arguments:
- psi: bfloat16 [16, 128, 2048], P('sector', 'mpo'), may hold values from -150 to 150
- left_env: bfloat16 [16, 128, 128, 128], P('sector', 'mpo'), may hold values from -0.5 to 0.5
- right_env: bfloat16 [16, 128, 128, 128], P('sector', 'mpo'), may hold values from -0.046875 to 0.046875
- term_op: int32 [128], P('mpo'), may hold values from 0 to 7
- ops: bfloat16 [8, 16, 16], replicated, may hold values from -1.5 to 1.5
- energy: float32 [16], replicated, may hold values from -2 to 2
- charge: int32 [16], P('sector'), may hold values from 0 to 15
- block_dims: int32 [16, 2], P('sector'), may hold values from 64 to 128, as said below
- basis: float32 [3, 16, 128, 2048], P(None, 'sector', 'mpo'), may hold values from -0.0029296875 to 0.0029296875
Outputs:
- hpsi: float32 [16, 128, 2048], P('sector', 'mpo')
- correction: float32 [16, 128, 2048], P('sector', 'mpo')
- ritz: float32 [], replicated
- subspace_row: float32 [3], replicated
Inputs may be any that keep to these rules, and one draw needn't show every extreme that they name: block_dims[s, 0] rows and block_dims[s, 1] columns of each padded block are valid; some block is full.
All inputs are finite; a program needn't handle non-finite values.
Results may differ from a plain program's by a relative error of at most 0.002.
Values may be sent and summed in bfloat16 or wider, within the bound.
A program may use at most 64 MiB of HBM per device.

v0:
```python
import math

import jax
import jax.numpy as jnp
from jax import lax
from jax.sharding import PartitionSpec as P


def sector_mask(block_dims, row_first, row_total, block_size, width):
    rows_ok = (row_first + jnp.arange(row_total, dtype=jnp.int32))[None, :, None] < block_dims[
        :, 0
    ][:, None, None]
    cols_ok = (jnp.arange(width, dtype=jnp.int32) % block_size)[None, None, :] < block_dims[:, 1][
        :, None, None
    ]
    return rows_ok & cols_ok


def block_terms(whole_x, left, right, op_mats, group, row_count):
    block_count = whole_x.shape[0]
    width = whole_x.shape[2]
    block_size = left.shape[-1]
    size_p = op_mats.shape[1]
    group_count = left.shape[1] // group

    def one_group(running, offset):
        left_part = lax.dynamic_slice(
            left, (0, offset, 0, 0), (block_count, group, row_count, block_size)
        )
        right_part = lax.dynamic_slice_in_dim(right, offset, group, 1)
        op_part = lax.dynamic_slice_in_dim(op_mats, offset, group, 0)
        moved = jnp.einsum(
            "skac,scq->skaq", left_part, whole_x, preferred_element_type=jnp.float32
        ).astype(jnp.bfloat16)
        moved = moved.reshape(block_count, group, row_count, size_p, block_size)
        mixed = jnp.einsum(
            "kpq,skaqb->skapb", op_part, moved, preferred_element_type=jnp.float32
        ).astype(jnp.bfloat16)
        running = running + jnp.einsum(
            "skapc,skcb->sapb", mixed, right_part, preferred_element_type=jnp.float32
        )
        return (running, None)

    offsets = jnp.arange(group_count, dtype=jnp.int32) * group
    running, _ = lax.scan(
        one_group, jnp.zeros((block_count, row_count, size_p, block_size), jnp.float32), offsets
    )
    return jnp.transpose(running.reshape(block_count, row_count, width), (1, 0, 2))


def body(psi, left_env, right_env, term_op, ops, energy, charge, block_dims, basis):
    block_size = left_env.shape[-1]
    local_rows = psi.shape[1]
    width = psi.shape[2]
    op_count = ops.shape[0]
    size_p = ops.shape[1]
    group = math.gcd(left_env.shape[1], 4)
    selector = (term_op[:, None] == jnp.arange(op_count, dtype=jnp.int32)[None, :]).astype(
        jnp.bfloat16
    )
    op_mats = jnp.dot(
        selector, ops.reshape(op_count, size_p * size_p), preferred_element_type=jnp.float32
    )
    op_mats = op_mats.astype(jnp.bfloat16).reshape(-1, size_p, size_p)
    full_mask = sector_mask(block_dims, 0, block_size, block_size, width)
    row_first = lax.axis_index("mpo") * local_rows
    own_mask = sector_mask(block_dims, row_first, local_rows, block_size, width)
    own_x = jnp.where(own_mask, psi, jnp.zeros_like(psi))
    gathered = lax.all_gather(psi, "mpo", axis=1, tiled=True)
    masked = jnp.where(full_mask, gathered, jnp.zeros_like(gathered))
    summed = lax.psum_scatter(
        block_terms(masked, left_env, right_env, op_mats, group, local_rows * lax.axis_size("mpo")),
        "mpo",
        scatter_dimension=0,
        tiled=True,
    )
    core = jnp.transpose(summed, (1, 0, 2))
    charge_hot = (charge[:, None] == jnp.arange(energy.shape[0], dtype=jnp.int32)[None, :]).astype(
        jnp.float32
    )
    level = jnp.sum(charge_hot * energy[None, :], axis=1)
    own_f = own_x.astype(jnp.float32)
    hpsi = jnp.where(own_mask, level[:, None, None] * own_f + core, jnp.zeros_like(core))
    self_sq = jnp.sum(own_f * own_f)
    cross = jnp.sum(own_f * hpsi)
    row_terms = jnp.sum(basis * hpsi[None], axis=(1, 2, 3))
    self_sq, cross, subspace_row = lax.psum((self_sq, cross, row_terms), ("sector", "mpo"))
    ritz = cross / (self_sq + 1e-06)
    resid = hpsi - ritz * own_f
    resid_sq = lax.psum(jnp.sum(resid * resid), ("sector", "mpo"))
    total_cells = psi.shape[0] * lax.axis_size("sector") * block_size * width
    correction = resid / jnp.sqrt(resid_sq / total_cells + 1e-06)
    return (hpsi, correction, ritz, subspace_row)


def solution(mesh):
    placed = (
        P("sector", "mpo", None),
        P("sector", "mpo", None, None),
        P("sector", "mpo", None, None),
        P("mpo"),
        P(),
        P(),
        P("sector"),
        P("sector", None),
        P(None, "sector", "mpo", None),
    )
    return jax.shard_map(
        body,
        mesh=mesh,
        in_specs=placed,
        out_specs=(P("sector", "mpo", None), P("sector", "mpo", None), P(), P()),
        check_vma=False,
    )
```

profile of v0, /device:TPU:0, one launch (start us, length us, event | category | flops | bytes accessed | tf_op | source)
XLA Modules:
  0.0 268.0 jit_solution(16876412433887006536)
XLA Ops:
  11.1 17.9 %all-gather.2.cloned.1.call-done = bf16[2,128,2048]{2,1,0:T(8,128)(2,1)} async-done(((bf16[2,32,2048]{2,1,0:T(8,128)(2,1)}), bf16[2,128,2048]{2,1,0:T(8,128)(2,1)}) %all-gather.2.cloned.1.call-update) | async-done | bytes 1048592 | tf_op jit(solution)/shard_map/all_gather | solution.py:69
  30.6 109.2 %while.11 = (s32[]{:T(128)}, f32[2,128,16,128]{3,1,2,0:T(8,128)S(1)}, s32[8]{0:T(128)S(1)}, bf16[2,32,128,128]{3,2,1,0:T(8,128)(2,1)}, bf16[2,128,2048]{2,1,0:T(...) while((s32[]{:T(128)}, ...), condition=%wide.region_2.3_spmd.clone, body=%wide.region_1.2_spmd.clone.sunk | while | flops 1146093568 | bytes 30949544 | solution.py:45
  33.2 2.2 convolution_convert_fusion.3
  36.8 3.2 %convert_bitcast_fusion.2 = bf16[2,4,128,16,128]{4,3,2,0,1:T(8,128)(2,1)} fusion(bf16[2,4,128,16,128]{4,3,2,1,0:T(8,128)(2,1)S(1)} %bitcast.54, bf16[32,16,16]{2,1,0:T(8,128)(2,1)S(1)} %get-tuple-element.171, s32[]{:T(128)S(6)} %select_n.52), kind=kOutput, calls=%fused_computation.4.clone.1 | convolution fusion | flops 69206016 | bytes 8404996 | tf_op jit(solution)/shard_map/while/body/eval_jaxpr/kpq,skaqb->skapb/dot_general | solution.py:36
  39.9 4.3 %bitcast_add_fusion.2 = f32[2,128,16,128]{3,1,2,0:T(8,128)S(1)} fusion(f32[2,128,16,128]{3,1,2,0:T(8,128)S(1)} %get-tuple-element.157, bf16[2,4,128,16,128]{4,3,2,0,1:T(8,128)(2,1)} %convert_bitcast_fusion.2, pred[]{:T(512)S(6)} %compare.4, bf16[2,32,128,128]{3,2,1,0:T(8,128)(2,1)} %get-tuple-element.172, s32[]{:T(128)S(6)} %select_n.52), kind=kOutput, calls=%fused_computation.6.clone.1 | convolution fusion | flops 537919488 | bytes 8650757 | tf_op jit(solution)/shard_map/while/body/eval_jaxpr/skapc,skcb->sapb/dot_general | solution.py:39
  46.8 2.2 convolution_convert_fusion.3
  50.4 3.2 %convert_bitcast_fusion.2 = bf16[2,4,128,16,128]{4,3,2,0,1:T(8,128)(2,1)} fusion(bf16[2,4,128,16,128]{4,3,2,1,0:T(8,128)(2,1)S(1)} %bitcast.54, bf16[32,16,16]{2,1,0:T(8,128)(2,1)S(1)} %get-tuple-element.171, s32[]{:T(128)S(6)} %select_n.52), kind=kOutput, calls=%fused_computation.4.clone.1 | convolution fusion | flops 69206016 | bytes 8404996 | tf_op jit(solution)/shard_map/while/body/eval_jaxpr/kpq,skaqb->skapb/dot_general | solution.py:36
  53.6 4.3 %bitcast_add_fusion.2 = f32[2,128,16,128]{3,1,2,0:T(8,128)S(1)} fusion(f32[2,128,16,128]{3,1,2,0:T(8,128)S(1)} %get-tuple-element.157, bf16[2,4,128,16,128]{4,3,2,0,1:T(8,128)(2,1)} %convert_bitcast_fusion.2, pred[]{:T(512)S(6)} %compare.4, bf16[2,32,128,128]{3,2,1,0:T(8,128)(2,1)} %get-tuple-element.172, s32[]{:T(128)S(6)} %select_n.52), kind=kOutput, calls=%fused_computation.6.clone.1 | convolution fusion | flops 537919488 | bytes 8650757 | tf_op jit(solution)/shard_map/while/body/eval_jaxpr/skapc,skcb->sapb/dot_general | solution.py:39
  60.5 2.2 convolution_convert_fusion.3
  64.1 3.2 %convert_bitcast_fusion.2 = bf16[2,4,128,16,128]{4,3,2,0,1:T(8,128)(2,1)} fusion(bf16[2,4,128,16,128]{4,3,2,1,0:T(8,128)(2,1)S(1)} %bitcast.54, bf16[32,16,16]{2,1,0:T(8,128)(2,1)S(1)} %get-tuple-element.171, s32[]{:T(128)S(6)} %select_n.52), kind=kOutput, calls=%fused_computation.4.clone.1 | convolution fusion | flops 69206016 | bytes 8404996 | tf_op jit(solution)/shard_map/while/body/eval_jaxpr/kpq,skaqb->skapb/dot_general | solution.py:36
  67.2 4.3 %bitcast_add_fusion.2 = f32[2,128,16,128]{3,1,2,0:T(8,128)S(1)} fusion(f32[2,128,16,128]{3,1,2,0:T(8,128)S(1)} %get-tuple-element.157, bf16[2,4,128,16,128]{4,3,2,0,1:T(8,128)(2,1)} %convert_bitcast_fusion.2, pred[]{:T(512)S(6)} %compare.4, bf16[2,32,128,128]{3,2,1,0:T(8,128)(2,1)} %get-tuple-element.172, s32[]{:T(128)S(6)} %select_n.52), kind=kOutput, calls=%fused_computation.6.clone.1 | convolution fusion | flops 537919488 | bytes 8650757 | tf_op jit(solution)/shard_map/while/body/eval_jaxpr/skapc,skcb->sapb/dot_general | solution.py:39
  77.7 3.2 %convert_bitcast_fusion.2 = bf16[2,4,128,16,128]{4,3,2,0,1:T(8,128)(2,1)} fusion(bf16[2,4,128,16,128]{4,3,2,1,0:T(8,128)(2,1)S(1)} %bitcast.54, bf16[32,16,16]{2,1,0:T(8,128)(2,1)S(1)} %get-tuple-element.171, s32[]{:T(128)S(6)} %select_n.52), kind=kOutput, calls=%fused_computation.4.clone.1 | convolution fusion | flops 69206016 | bytes 8404996 | tf_op jit(solution)/shard_map/while/body/eval_jaxpr/kpq,skaqb->skapb/dot_general | solution.py:36
  80.9 4.3 %bitcast_add_fusion.2 = f32[2,128,16,128]{3,1,2,0:T(8,128)S(1)} fusion(f32[2,128,16,128]{3,1,2,0:T(8,128)S(1)} %get-tuple-element.157, bf16[2,4,128,16,128]{4,3,2,0,1:T(8,128)(2,1)} %convert_bitcast_fusion.2, pred[]{:T(512)S(6)} %compare.4, bf16[2,32,128,128]{3,2,1,0:T(8,128)(2,1)} %get-tuple-element.172, s32[]{:T(128)S(6)} %select_n.52), kind=kOutput, calls=%fused_computation.6.clone.1 | convolution fusion | flops 537919488 | bytes 8650757 | tf_op jit(solution)/shard_map/while/body/eval_jaxpr/skapc,skcb->sapb/dot_general | solution.py:39
  91.4 3.2 %convert_bitcast_fusion.2 = bf16[2,4,128,16,128]{4,3,2,0,1:T(8,128)(2,1)} fusion(bf16[2,4,128,16,128]{4,3,2,1,0:T(8,128)(2,1)S(1)} %bitcast.54, bf16[32,16,16]{2,1,0:T(8,128)(2,1)S(1)} %get-tuple-element.171, s32[]{:T(128)S(6)} %select_n.52), kind=kOutput, calls=%fused_computation.4.clone.1 | convolution fusion | flops 69206016 | bytes 8404996 | tf_op jit(solution)/shard_map/while/body/eval_jaxpr/kpq,skaqb->skapb/dot_general | solution.py:36
  94.5 4.3 %bitcast_add_fusion.2 = f32[2,128,16,128]{3,1,2,0:T(8,128)S(1)} fusion(f32[2,128,16,128]{3,1,2,0:T(8,128)S(1)} %get-tuple-element.157, bf16[2,4,128,16,128]{4,3,2,0,1:T(8,128)(2,1)} %convert_bitcast_fusion.2, pred[]{:T(512)S(6)} %compare.4, bf16[2,32,128,128]{3,2,1,0:T(8,128)(2,1)} %get-tuple-element.172, s32[]{:T(128)S(6)} %select_n.52), kind=kOutput, calls=%fused_computation.6.clone.1 | convolution fusion | flops 537919488 | bytes 8650757 | tf_op jit(solution)/shard_map/while/body/eval_jaxpr/skapc,skcb->sapb/dot_general | solution.py:39
  105.0 3.2 %convert_bitcast_fusion.2 = bf16[2,4,128,16,128]{4,3,2,0,1:T(8,128)(2,1)} fusion(bf16[2,4,128,16,128]{4,3,2,1,0:T(8,128)(2,1)S(1)} %bitcast.54, bf16[32,16,16]{2,1,0:T(8,128)(2,1)S(1)} %get-tuple-element.171, s32[]{:T(128)S(6)} %select_n.52), kind=kOutput, calls=%fused_computation.4.clone.1 | convolution fusion | flops 69206016 | bytes 8404996 | tf_op jit(solution)/shard_map/while/body/eval_jaxpr/kpq,skaqb->skapb/dot_general | solution.py:36
  108.2 4.3 %bitcast_add_fusion.2 = f32[2,128,16,128]{3,1,2,0:T(8,128)S(1)} fusion(f32[2,128,16,128]{3,1,2,0:T(8,128)S(1)} %get-tuple-element.157, bf16[2,4,128,16,128]{4,3,2,0,1:T(8,128)(2,1)} %convert_bitcast_fusion.2, pred[]{:T(512)S(6)} %compare.4, bf16[2,32,128,128]{3,2,1,0:T(8,128)(2,1)} %get-tuple-element.172, s32[]{:T(128)S(6)} %select_n.52), kind=kOutput, calls=%fused_computation.6.clone.1 | convolution fusion | flops 537919488 | bytes 8650757 | tf_op jit(solution)/shard_map/while/body/eval_jaxpr/skapc,skcb->sapb/dot_general | solution.py:39
  118.7 3.2 %convert_bitcast_fusion.2 = bf16[2,4,128,16,128]{4,3,2,0,1:T(8,128)(2,1)} fusion(bf16[2,4,128,16,128]{4,3,2,1,0:T(8,128)(2,1)S(1)} %bitcast.54, bf16[32,16,16]{2,1,0:T(8,128)(2,1)S(1)} %get-tuple-element.171, s32[]{:T(128)S(6)} %select_n.52), kind=kOutput, calls=%fused_computation.4.clone.1 | convolution fusion | flops 69206016 | bytes 8404996 | tf_op jit(solution)/shard_map/while/body/eval_jaxpr/kpq,skaqb->skapb/dot_general | solution.py:36
  121.8 4.3 %bitcast_add_fusion.2 = f32[2,128,16,128]{3,1,2,0:T(8,128)S(1)} fusion(f32[2,128,16,128]{3,1,2,0:T(8,128)S(1)} %get-tuple-element.157, bf16[2,4,128,16,128]{4,3,2,0,1:T(8,128)(2,1)} %convert_bitcast_fusion.2, pred[]{:T(512)S(6)} %compare.4, bf16[2,32,128,128]{3,2,1,0:T(8,128)(2,1)} %get-tuple-element.172, s32[]{:T(128)S(6)} %select_n.52), kind=kOutput, calls=%fused_computation.6.clone.1 | convolution fusion | flops 537919488 | bytes 8650757 | tf_op jit(solution)/shard_map/while/body/eval_jaxpr/skapc,skcb->sapb/dot_general | solution.py:39
  132.3 3.2 %convert_bitcast_fusion.2 = bf16[2,4,128,16,128]{4,3,2,0,1:T(8,128)(2,1)} fusion(bf16[2,4,128,16,128]{4,3,2,1,0:T(8,128)(2,1)S(1)} %bitcast.54, bf16[32,16,16]{2,1,0:T(8,128)(2,1)S(1)} %get-tuple-element.171, s32[]{:T(128)S(6)} %select_n.52), kind=kOutput, calls=%fused_computation.4.clone.1 | convolution fusion | flops 69206016 | bytes 8404996 | tf_op jit(solution)/shard_map/while/body/eval_jaxpr/kpq,skaqb->skapb/dot_general | solution.py:36
  135.5 4.3 %bitcast_add_fusion.2 = f32[2,128,16,128]{3,1,2,0:T(8,128)S(1)} fusion(f32[2,128,16,128]{3,1,2,0:T(8,128)S(1)} %get-tuple-element.157, bf16[2,4,128,16,128]{4,3,2,0,1:T(8,128)(2,1)} %convert_bitcast_fusion.2, pred[]{:T(512)S(6)} %compare.4, bf16[2,32,128,128]{3,2,1,0:T(8,128)(2,1)} %get-tuple-element.172, s32[]{:T(128)S(6)} %select_n.52), kind=kOutput, calls=%fused_computation.6.clone.1 | convolution fusion | flops 537919488 | bytes 8650757 | tf_op jit(solution)/shard_map/while/body/eval_jaxpr/skapc,skcb->sapb/dot_general | solution.py:39
  142.4 30.7 %reduce-scatter.2.cloned.1.call-done = f32[32,2,2048]{2,0,1:T(8,128)} async-done(((f32[128,2,2048]{2,0,1:T(8,128)}), f32[32,2,2048]{2,0,1:T(8,128)}) %reduce-scatter.2.cloned.1.call-update) | async-done | bytes 524304 | tf_op jit(solution)/shard_map/reduce_scatter | solution.py:71
  175.0 39.6 %all-reduce.1 = (f32[]{:T(128)}, f32[]{:T(128)}) all-reduce(f32[]{:T(128)} %get-tuple-element.81, f32[]{:T(128)} %get-tuple-element.80), channel_id=1, replica_groups=mesh['sector'=8,'mpo'=4] {'sector','mpo'}, use_global_device_ids=true, to_apply=%region_5.6 | all-reduce | flops 2 | bytes 16 | tf_op jit(solution)/shard_map/psum | solution.py:87
  217.0 41.4 %all-reduce = (f32[]{:T(128)}, f32[3]{0:T(128)}) all-reduce(f32[]{:T(128)} %multiply_reduce_fusion.1, f32[3]{0:T(128)S(1)} %multiply_reduce_fusion), channel_id=1, replica_groups=mesh['sector'=8,'mpo'=4] {'sector','mpo'}, use_global_device_ids=true, to_apply=%region_9.10 | all-reduce | flops 4 | bytes 32 | tf_op jit(solution)/shard_map/psum | solution.py:90
  (54 shorter events, 39.0 us)
Async XLA Ops:
  7.2 21.9 %all-gather.2.cloned.1.call-start = ((), (), s32[]{:S(2)}) async-start(), calls=%async_computation.1 | async-start | bytes 1310720 | tf_op jit(solution)/shard_map/all_gather | solution.py:69
  7.9 165.2 %reduce-scatter.2.cloned.1.call-start = ((), (), s32[]{:S(2)}) async-start(), calls=%async_computation.2 | async-start | bytes 2621440 | tf_op jit(solution)/shard_map/reduce_scatter | solution.py:71
  141.4 0.7 copy-start.3
  141.4 0.7 copy-start.4
  141.4 31.6 %copy-start.1 = (bf16[2,32,2048]{2,1,0:T(8,128)(2,1)S(1)}, bf16[2,32,2048]{2,1,0:T(8,128)(2,1)}, u32[]{:S(2)}) copy-start(bf16[2,32,2048]{2,1,0:T(8,128)(2,1)} %param.11) | copy-start | bytes 786436
  141.4 74.4 %copy-start.2 = (f32[3,2,32,2048]{3,2,1,0:T(8,128)S(1)}, f32[3,2,32,2048]{3,2,1,0:T(8,128)}, u32[]{:S(2)}) copy-start(f32[3,2,32,2048]{3,2,1,0:T(8,128)} %param.19) | copy-start | bytes 4718596
  175.0 85.1 %copy-start = (f32[2,32,2048]{2,1,0:T(8,128)}, f32[2,32,2048]{2,1,0:T(8,128)S(1)}, u32[]{:S(2)}) copy-start(f32[2,32,2048]{2,1,0:T(8,128)S(1)} %get-tuple-element.102) | copy-start | bytes 1572868
Sparse Core Ops, SparseCore 0:
  9.6 19.4 all-gather.1
  141.6 31.4 reduce-scatter.1
where the time goes:
time: 269 us; the launch traced here: 268 us
  blocking collectives  81 us (30%)
  matrix products  78.2 us (29%)
  waiting for transfers between devices  49.3 us (18%)
  local copies, waits for them, and re-layouts  20.3 us (8%)
  between operations  17.3 us (6%)
  loops' own time  15.9 us (6%)
  other arithmetic  6.02 us (2%)
    psum x1, blocking collectives, body(): resid_sq = lax.psum(jnp.sum(resid * resid), ('sector', 'mpo'))  41.4 us
    psum x1, blocking collectives, body(): lax.psum((self_sq, cross, row_terms), ('sector', 'mpo'))  39.6 us
    dot_general x8, matrix products, one_group(): jnp.einsum('skapc,skcb->sapb', mixed, right_part, preferred_element_type=...  34.5 us
    reduce_scatter x1, waiting for transfers between devices, body(): lax.psum_scatter(block_terms(masked, left_env, right_env, op_mats, group,...  30.7 us
    dot_general x8, matrix products, one_group(): jnp.einsum('kpq,skaqb->skapb', op_part, moved, preferred_element_type=jnp...  25.3 us
    all_gather x1, waiting for transfers between devices, body(): gathered = lax.all_gather(psi, 'mpo', axis=1, tiled=True)  17.9 us
    dot_general x8, matrix products, one_group(): jnp.einsum('skac,scq->skaq', left_part, whole_x, preferred_element_type=j...  17.6 us
    another operation x1, loops' own time, block_terms(): lax.scan(one_group, jnp.zeros((block_count, row_count, size_p, block_size...  15.9 us
  transfers between devices with their start and end apart: 2, of which 2 were waited for; matrix products, arithmetic and copies ran while one was open for 1% of the time, Pallas kernels for 0%

commit v1 on v0

v1 whole, which is shorter than its diff:
```python
import functools

import jax
import jax.numpy as jnp
from jax import lax
from jax.experimental import pallas as pl
from jax.experimental.pallas import tpu as pltpu
from jax.sharding import PartitionSpec as P

MESH = pl.DeviceIdType.MESH


def gather_kernel(n, sectors, psi_ref, out_ref, own_sem, send, recv, fsend, frecv):
    row = lax.axis_index("sector")
    me = lax.axis_index("mpo")
    chips = n // 2
    core, chip = lax.rem(me, 2), lax.div(me, 2)
    sib = chip * 2 + 1 - core

    def at(hop):
        return lax.rem(chip + hop, chips) * 2

    barrier = pltpu.get_barrier_semaphore()
    for hop in range(1, chips):
        pl.semaphore_signal(barrier, inc=1, device_id=(row, at(hop) + core), device_id_type=MESH)
    pl.semaphore_signal(barrier, inc=1, device_id=(row, sib), device_id_type=MESH)
    pl.semaphore_wait(barrier, chips)

    def push(src, block, s, to, ssem, rsem):
        return pltpu.make_async_remote_copy(
            src_ref=src,
            dst_ref=out_ref.at[block, s],
            send_sem=ssem,
            recv_sem=rsem,
            device_id=(row, to),
            device_id_type=MESH,
        )

    far, near, relay = {}, {}, {}
    for s in range(sectors):
        for hop in range(1, chips):
            far[hop, s] = push(
                psi_ref.at[s], me, s, at(hop) + core, send.at[hop, s], recv.at[hop, s]
            )
            far[hop, s].start()
    for s in range(sectors):
        near[s] = push(psi_ref.at[s], me, s, sib, send.at[0, s], recv.at[0, s])
        near[s].start()
    own = pltpu.make_async_copy(psi_ref, out_ref.at[me], own_sem)
    own.start()
    for s in range(sectors):
        for hop in range(1, chips):
            far[hop, s].wait_recv()
            block = at(chips - hop) + core
            relay[hop, s] = push(
                out_ref.at[block, s], block, s, sib, fsend.at[hop, s], frecv.at[hop, s]
            )
            relay[hop, s].start()
    own.wait()
    for s in range(sectors):
        near[s].wait()
        for hop in range(1, chips):
            far[hop, s].wait_send()
            relay[hop, s].wait()


def gather(psi, n):
    sectors, rows, width = psi.shape
    chips = n // 2
    return pl.pallas_call(
        functools.partial(gather_kernel, n, sectors),
        out_shape=jax.ShapeDtypeStruct((n, sectors, rows, width), psi.dtype),
        in_specs=[pl.BlockSpec(memory_space=pl.ANY)],
        out_specs=pl.BlockSpec(memory_space=pl.ANY),
        scratch_shapes=[pltpu.SemaphoreType.DMA(())]
        + [pltpu.SemaphoreType.DMA((chips, sectors))] * 4,
        compiler_params=pltpu.CompilerParams(collective_id=0, has_side_effects=True),
        name="gather",
    )(psi)


def terms_kernel(
    size_p, op_ref, opmat_ref, x_ref, left_ref, right_ref, out_ref, sums, count, first, lists
):
    terms = left_ref.shape[1]
    blk = left_ref.shape[2]
    op_count = count.shape[0]
    slots = lists.shape[1]

    for o in range(op_count):
        count[o] = 0

    def tally(k, c):
        o = op_ref[k]
        count[o] = count[o] + 1
        return c

    lax.fori_loop(0, terms, tally, 0)
    total = jnp.int32(0)
    for o in range(op_count):
        first[o] = total * 2
        total = total + lax.div(count[o] + 1, 2)

    def clear(i, c):
        lists[0, i] = 0
        lists[1, i] = 0
        lists[2, i] = 0
        return c

    lax.fori_loop(0, slots, clear, 0)

    def place(k, c):
        o = op_ref[k]
        spot = first[o]
        first[o] = spot + 1
        lists[0, spot] = k
        lists[1, spot] = 1
        lists[2, lax.div(spot, 2)] = o
        return c

    lax.fori_loop(0, terms, place, 0)

    sums[...] = jnp.zeros_like(sums)

    def pair(i, c):
        k1, k2 = lists[0, 2 * i], lists[0, 2 * i + 1]
        used = lists[1, 2 * i + 1]
        o = lists[2, i]
        left = jnp.concatenate([left_ref[0, k1], left_ref[0, k2]], axis=0)
        second = right_ref[0, k2]
        second = jnp.where(used > 0, second, jnp.zeros_like(second))
        right = jnp.concatenate([right_ref[0, k1], second], axis=0)
        step = 2
        for t in range(size_p // step):
            cols = pl.ds(t * step * blk, step * blk)
            v = jnp.dot(left, x_ref[0, :, cols], preferred_element_type=jnp.float32)
            v = v.astype(jnp.bfloat16)
            both = [
                jnp.concatenate(
                    [v[:blk, u * blk : (u + 1) * blk], v[blk:, u * blk : (u + 1) * blk]], axis=1
                )
                for u in range(step)
            ]
            both = jnp.concatenate(both, axis=0)
            start = pl.multiple_of(o * size_p * blk, blk) + t * step * blk
            rows = pl.ds(pl.multiple_of(start, blk), step * blk)
            sums[rows, :] = sums[rows, :] + jnp.dot(
                both, right, preferred_element_type=jnp.float32
            )
        return c

    lax.fori_loop(0, total, pair, 0)

    opmat = opmat_ref[...]
    depth = op_count * size_p

    def mix(i, c):
        for u in range(4):
            a = i * 8 + u * 2
            y = jnp.concatenate(
                [sums[pl.ds(a, depth, stride=blk), :], sums[pl.ds(a + 1, depth, stride=blk), :]],
                axis=1,
            )
            high = y.astype(jnp.bfloat16)
            low = (y - high.astype(jnp.float32)).astype(jnp.bfloat16)
            m = jnp.dot(
                opmat,
                jnp.concatenate([high, low], axis=0),
                preferred_element_type=jnp.float32,
            )
            base = pl.multiple_of(i * 8 * size_p, size_p) + u * 2 * size_p
            base = pl.multiple_of(base, size_p)
            out_ref[0, pl.ds(base, size_p), :] = m[:, :blk]
            out_ref[0, pl.ds(pl.multiple_of(base + size_p, size_p), size_p), :] = m[:, blk:]
        return c

    lax.fori_loop(0, blk // 8, mix, 0)


def local_terms(x, left, right, term_op, ops):
    sectors, terms, blk, _ = left.shape
    op_count, size_p, _ = ops.shape
    width = x.shape[2]
    opmat = jnp.transpose(ops, (1, 0, 2)).reshape(size_p, op_count * size_p)
    opmat = jnp.concatenate([opmat, opmat], axis=1)
    flops = 4 * sectors * terms * blk * blk * width
    return pl.pallas_call(
        functools.partial(terms_kernel, size_p),
        out_shape=jax.ShapeDtypeStruct((sectors, blk * size_p, blk), jnp.float32),
        grid=(sectors,),
        in_specs=[
            pl.BlockSpec(memory_space=pltpu.SMEM),
            pl.BlockSpec(opmat.shape, lambda s: (0, 0)),
            pl.BlockSpec((1, blk, width), lambda s: (s, 0, 0)),
            pl.BlockSpec((1, terms, blk, blk), lambda s: (s, 0, 0, 0)),
            pl.BlockSpec((1, terms, blk, blk), lambda s: (s, 0, 0, 0)),
        ],
        out_specs=pl.BlockSpec((1, blk * size_p, blk), lambda s: (s, 0, 0)),
        scratch_shapes=[
            pltpu.VMEM((op_count * size_p * blk, blk), jnp.float32),
            pltpu.SMEM((op_count,), jnp.int32),
            pltpu.SMEM((op_count,), jnp.int32),
            pltpu.SMEM((3, terms + op_count + 2), jnp.int32),
        ],
        compiler_params=pltpu.CompilerParams(vmem_limit_bytes=44 * 2**20),
        cost_estimate=pl.CostEstimate(
            flops=flops, bytes_accessed=4 * sectors * terms * blk * blk, transcendentals=0
        ),
        name="terms",
    )(term_op, opmat, x, left, right)


def merge(stats, nb):
    xx, xh = stats[:, 0:1], stats[:, 1:2]
    rr, xr = stats[:, 2 + nb : 3 + nb], stats[:, 3 + nb : 4 + nb]
    q = xh / (xx + 1e-6)
    total = jnp.sum(stats, axis=0)
    all_q = total[1:2] / (total[0:1] + 1e-6)
    gap = q - all_q[None]
    rr = jnp.sum(rr + 2.0 * gap * xr + gap * gap * xx, axis=0)
    xr = jnp.sum(xr + gap * xx, axis=0)
    return jnp.concatenate(
        [total[: 2 + nb], rr, xr, jnp.zeros((4 - nb, total.shape[1]), jnp.float32)], axis=0
    ), all_q


def finish_kernel(
    n,
    groups,
    cells,
    dims_ref,
    level_ref,
    part_ref,
    psi_ref,
    basis_hbm,
    hpsi_ref,
    corr_ref,
    stat_ref,
    basis_ref,
    mine,
    theirs,
    landed,
    slots_m,
    slots_s,
    tile,
    basis_sem,
    load_sem,
    send1,
    recv1,
    send2,
    recv2,
    send3,
    recv3,
):
    row = lax.axis_index("sector")
    me = lax.axis_index("mpo")
    chips = n // 2
    core, chip = lax.rem(me, 2), lax.div(me, 2)
    sib = chip * 2 + 1 - core
    sectors, rows, width = psi_ref.shape
    nb = basis_ref.shape[0]
    blk = part_ref.shape[2]
    size_p = width // blk
    chunk = rows * size_p

    barrier = pltpu.get_barrier_semaphore()
    for j in range(1, n):
        pl.semaphore_signal(
            barrier, inc=1, device_id=(row, lax.rem(me + j, n)), device_id_type=MESH
        )
    for j in range(1, groups):
        pl.semaphore_signal(
            barrier, inc=1, device_id=(lax.rem(row + j, groups), me), device_id_type=MESH
        )
    basis_copy = pltpu.make_async_copy(basis_hbm, basis_ref, basis_sem)
    pl.semaphore_wait(barrier, n + groups - 2)

    def part(hop, which, s):
        block = lax.rem(chip + hop, chips) * 2 + which
        return part_ref.at[s, pl.ds(pl.multiple_of(block * chunk, chunk), chunk)]

    order = list(range(1, chips)) + [0]
    loads, swaps, sends = {}, {}, {}
    for hop in order:
        for s in range(sectors):
            swaps[hop, s] = pltpu.make_async_remote_copy(
                src_ref=part(hop, 1 - core, s),
                dst_ref=theirs.at[hop, s],
                send_sem=send1.at[hop, s],
                recv_sem=recv1.at[hop, s],
                device_id=(row, sib),
                device_id_type=MESH,
            )
            swaps[hop, s].start()
            loads[hop, s] = pltpu.make_async_copy(
                part(hop, core, s), mine.at[hop, s], load_sem.at[hop, s]
            )
            loads[hop, s].start()
    basis_copy.start()
    for hop in order:
        for s in range(sectors):
            loads[hop, s].wait()
            swaps[hop, s].wait_recv()
            mine[hop, s] = mine[hop, s] + theirs[hop, s]
            if hop:
                sends[hop, s] = pltpu.make_async_remote_copy(
                    src_ref=mine.at[hop, s],
                    dst_ref=landed.at[hop - 1, s],
                    send_sem=send2.at[hop, s],
                    recv_sem=recv2.at[hop, s],
                    device_id=(row, lax.rem(chip + hop, chips) * 2 + core),
                    device_id_type=MESH,
                )
                sends[hop, s].start()
    basis_copy.wait()

    row_at = me * rows + lax.broadcasted_iota(jnp.int32, (rows, blk), 0)
    col_at = lax.broadcasted_iota(jnp.int32, (rows, blk), 1)
    zero = jnp.zeros((rows, blk), jnp.float32)
    xx, xh, bh = zero, zero, [zero] * nb
    for s in range(sectors):
        for hop in range(1, chips):
            sends[hop, s].wait_recv()
        mask = (row_at < dims_ref[s, 0]) & (col_at < dims_ref[s, 1])
        level = level_ref[s]
        for p in range(size_p):
            cols = slice(p * blk, (p + 1) * blk)
            spots = pl.ds(p, rows, stride=size_p)
            core_p = mine[0, s, spots, :]
            for hop in range(1, chips):
                core_p = core_p + landed[hop - 1, s, spots, :]
            x = jnp.where(mask, psi_ref[s, :, cols].astype(jnp.float32), zero)
            h = jnp.where(mask, level * x + core_p, zero)
            hpsi_ref[s, :, cols] = h
            corr_ref[s, :, cols] = x
            xx = xx + x * x
            xh = xh + x * h
            bh = [bh[j] + basis_ref[j, s, :, cols] * h for j in range(nb)]

    def whole(v):
        v = jnp.sum(jnp.sum(v, axis=0, keepdims=True), axis=1, keepdims=True)
        return jnp.broadcast_to(v, (1, blk))

    xx, xh, bh = whole(xx), whole(xh), [whole(b) for b in bh]
    q = xh / (xx + 1e-6)
    rr, xr = zero, zero
    for s in range(sectors):
        for p in range(size_p):
            cols = slice(p * blk, (p + 1) * blk)
            x = corr_ref[s, :, cols]
            r = hpsi_ref[s, :, cols] - q * x
            rr = rr + r * r
            xr = xr + x * r
    stats = jnp.concatenate(
        [xx, xh] + bh + [whole(rr), whole(xr), jnp.zeros((4 - nb, blk), jnp.float32)], axis=0
    )

    def spread(level_no, stats, slots, count, mine_at, target):
        tile[level_no] = stats
        slots[mine_at] = stats
        for j in range(1, count):
            pltpu.make_async_remote_copy(
                src_ref=tile.at[level_no],
                dst_ref=slots.at[mine_at],
                send_sem=send3.at[level_no],
                recv_sem=recv3.at[level_no],
                device_id=target(j),
                device_id_type=MESH,
            ).start()
        some = slots.at[pl.ds(0, count - 1)]
        pltpu.make_async_copy(some, some, recv3.at[level_no]).wait()
        pltpu.make_async_copy(some, some, send3.at[level_no]).wait()
        return merge(slots[...], nb)

    stats, q = spread(0, stats, slots_m, n, me, lambda j: (row, lax.rem(me + j, n)))
    stats, q = spread(1, stats, slots_s, groups, row, lambda j: (lax.rem(row + j, groups), me))
    stat_ref[...] = jnp.concatenate([q, stats[1:]], axis=0)
    scale = 1.0 / jnp.sqrt(stats[2 + nb : 3 + nb] / cells + 1e-6)
    for s in range(sectors):
        for p in range(size_p):
            cols = slice(p * blk, (p + 1) * blk)
            corr_ref[s, :, cols] = (hpsi_ref[s, :, cols] - q * corr_ref[s, :, cols]) * scale
    for s in range(sectors):
        for hop in order:
            swaps[hop, s].wait_send()
            if hop:
                sends[hop, s].wait_send()


def finish(parts, psi, basis, dims, level, n, groups):
    sectors, rows, width = psi.shape
    nb = basis.shape[0]
    blk = parts.shape[2]
    chips = n // 2
    chunk = rows * (width // blk)
    cells = float(sectors * groups * rows * n * width)
    smem = pl.BlockSpec(memory_space=pltpu.SMEM)
    vmem = pl.BlockSpec(memory_space=pltpu.VMEM)
    far = pl.BlockSpec(memory_space=pl.ANY)
    dma = pltpu.SemaphoreType.DMA
    like = jax.ShapeDtypeStruct(psi.shape, jnp.float32)
    return pl.pallas_call(
        functools.partial(finish_kernel, n, groups, cells),
        out_shape=(like, like, jax.ShapeDtypeStruct((8, blk), jnp.float32)),
        in_specs=[smem, smem, far, vmem, far],
        out_specs=(vmem, vmem, vmem),
        scratch_shapes=[
            pltpu.VMEM(basis.shape, jnp.float32),
            pltpu.VMEM((chips, sectors, chunk, blk), jnp.float32),
            pltpu.VMEM((chips, sectors, chunk, blk), jnp.float32),
            pltpu.VMEM((max(chips - 1, 1), sectors, chunk, blk), jnp.float32),
            pltpu.VMEM((n, 8, blk), jnp.float32),
            pltpu.VMEM((groups, 8, blk), jnp.float32),
            pltpu.VMEM((2, 8, blk), jnp.float32),
            dma(()),
            dma((chips, sectors)),
            dma((chips, sectors)),
            dma((chips, sectors)),
            dma((chips, sectors)),
            dma((chips, sectors)),
            dma((2,)),
            dma((2,)),
        ],
        compiler_params=pltpu.CompilerParams(
            collective_id=1, has_side_effects=True, vmem_limit_bytes=32 * 2**20
        ),
        name="finish",
    )(dims, level, parts, psi, basis)


def body(n, groups, psi, left_env, right_env, term_op, ops, energy, charge, block_dims, basis):
    blk = left_env.shape[-1]
    sectors, rows, width = psi.shape
    x = jnp.transpose(gather(psi, n), (1, 0, 2, 3)).reshape(sectors, n * rows, width)
    rows_ok = jnp.arange(blk, dtype=jnp.int32)[None, :, None] < block_dims[:, 0][:, None, None]
    cols_ok = (jnp.arange(width, dtype=jnp.int32) % blk)[None, None, :] < block_dims[:, 1][
        :, None, None
    ]
    x = jnp.where(rows_ok & cols_ok, x, jnp.zeros_like(x))
    parts = local_terms(x, left_env, right_env, term_op, ops)
    hot = (charge[:, None] == jnp.arange(energy.shape[0], dtype=jnp.int32)[None, :]).astype(
        jnp.float32
    )
    level = jnp.sum(hot * energy[None, :], axis=1)
    hpsi, correction, stats = finish(parts, psi, basis, block_dims, level, n, groups)
    return (hpsi, correction, stats[0, 0], stats[2 : 2 + basis.shape[0], 0])


def solution(mesh):
    placed = (
        P("sector", "mpo", None),
        P("sector", "mpo", None, None),
        P("sector", "mpo", None, None),
        P("mpo"),
        P(),
        P(),
        P("sector"),
        P("sector", None),
        P(None, "sector", "mpo", None),
    )
    return jax.shard_map(
        functools.partial(body, mesh.shape["mpo"], mesh.shape["sector"]),
        mesh=mesh,
        in_specs=placed,
        out_specs=(P("sector", "mpo", None), P("sector", "mpo", None), P(), P()),
        check_vma=False,
    )
```

time: 269 us -> 95.3 us (0.35)
  Pallas kernels: 0 us -> 87 us
  blocking collectives: 81 us -> 0 us
  matrix products: 78.2 us -> 0 us
  waiting for transfers between devices: 49.3 us -> 0 us
  between operations: 17.3 us -> 0.77 us
  loops' own time: 15.9 us -> 0 us
  local copies, waits for them, and re-layouts: 20.3 us -> 6.89 us
  other arithmetic: 6.02 us -> 0.72 us
    pallas_call x0 -> x3, Pallas kernels: none -> 87 us  [the longest x1 49.4 us: local_terms(): pl.pallas_call(functools.partial(terms_kernel, size_p), out_shape=jax.Sha...]
    psum x2 -> x0, blocking collectives: 81 us -> none  [the longest x1 41.4 us: body(): resid_sq = lax.psum(jnp.sum(resid * resid), ('sector', 'mpo'))]
    dot_general x25 -> x0, matrix products: 78.2 us -> none  [the longest x8 34.5 us: one_group(): jnp.einsum('skapc,skcb->sapb', mixed, right_part, preferred_element_type=...]
    reduce_scatter x1 -> x0, waiting for transfers between devices: 30.7 us -> none  [body(): lax.psum_scatter(block_terms(masked, left_env, right_env, op_mats, group,...]
    all_gather x1 -> x0, waiting for transfers between devices: 17.9 us -> none  [body(): gathered = lax.all_gather(psi, 'mpo', axis=1, tiled=True)]
    another operation x1 -> x0, loops' own time: 15.9 us -> none  [block_terms(): lax.scan(one_group, jnp.zeros((block_count, row_count, size_p, block_size...]
    while x8 -> x0, local copies, waits for them, and re-layouts: 11.3 us -> none
    dynamic_slice x8 -> x0, local copies, waits for them, and re-layouts: 4.69 us -> none  [block_terms(): lax.scan(one_group, jnp.zeros((block_count, row_count, size_p, block_size...]
  transfers between devices with their start and end apart: 2 -> 0, of which waited for: 2 -> 0; matrix products, arithmetic and copies ran while one was open for 1% -> 0% of each run, Pallas kernels for 0% -> 0%
where the time goes in v1:
time: 95.3 us; the launch traced here: 95.4 us
  Pallas kernels  87 us (91%)
  local copies, waits for them, and re-layouts  6.89 us (7%)
    pallas_call x1, Pallas kernels, local_terms(): pl.pallas_call(functools.partial(terms_kernel, size_p), out_shape=jax.Sha...  49.4 us
    pallas_call x1, Pallas kernels, finish(): pl.pallas_call(functools.partial(finish_kernel, n, groups, cells), out_sh...  25.5 us
    pallas_call x1, Pallas kernels, gather(): pl.pallas_call(functools.partial(gather_kernel, n, sectors), out_shape=ja...  12.1 us
    unnamed x20, local copies, waits for them, and re-layouts  3.21 us

profile of v1, /device:TPU:0, one launch (start us, length us, event | category | flops | bytes accessed | tf_op | source)
XLA Modules:
  0.0 95.4 jit_solution(11213801196248496241)
XLA Ops:
  0.6 1.0 %slice_reduce_fusion.2 = (s32[2]{0:T(128)S(1)}, s32[2]{0:T(128)S(1)}) fusion(s32[2,2]{1,0:T(2,128)} %dims_ref.1), kind=kLoop, calls=%fused_computation.12 | loop fusion | bytes 32 | tf_op jit(solution)/shard_map/slice | solution.py:435
  1.6 0.1 broadcast_compare_fusion
  1.7 0.1 iota_compare_fusion
  1.8 12.1 %gather.1 = bf16[4,2,32,2048]{3,2,1,0:T(8,128)(2,1)} custom-call(bf16[2,32,2048]{2,1,0:T(8,128)(2,1)} %psi_ref.3), custom_call_target="tpu_custom_call" | custom-call | tf_op jit(solution)/shard_map/gather/pallas_call | solution.py:70
  13.9 0.0 copy-start.6
  13.9 0.0 copy-start.3
  13.9 0.0 copy-start.5
  14.0 1.5 %copy.18 = bf16[2,4,32,2048]{3,2,1,0:T(8,128)(2,1)S(1)} copy(bf16[2,4,32,2048]{3,2,0,1:T(8,128)(2,1)} %bitcast.5) | data formatting | bytes 2097152 | tf_op jit(solution)/shard_map/transpose | solution.py:434
  15.4 0.4 and_select_fusion.x_ref
  15.8 0.0 copy-done.6
  15.8 0.1 reshape.83
  16.0 0.0 copy-done.5
  16.0 0.0 copy-start.4
  16.0 1.6 %copy-done.4 = bf16[2,32,128,128]{3,2,1,0:T(8,128)(2,1)S(1)} copy-done((bf16[2,32,128,128]{3,2,1,0:T(8,128)(2,1)S(1)}, bf16[2,32,128,128]{3,2,1,0:T(8,128)(2,1)}, u32[]{:S(2)}) %copy-start.4) | copy-done | bytes 2097176
  17.6 0.0 copy-start.2
  17.6 49.4 %terms.1.part_ref = f32[2,2048,128]{2,1,0:T(8,128)S(1)} custom-call(s32[32]{0:T(128)S(1)} %copy-done.5, bf16[16,256]{1,0:T(8,128)(2,1)S(1)} %pad_maximum_fusion.opmat_ref, bf16[2,128,2048]{2,1,0:T(8,128)(2,1)S(1)} %and_select_fusion.x_ref, bf16[2,32,128,128]{3,2,1,0:T(8,128)(2,1)S(1)} %copy-done.3, bf16[2,32,128,128]{3,2,1,0:T(8,128)(2,1)S(1)} %copy-done.4), custom_call_target="tpu_custom_call" | custom-call | flops 8589934592 | bytes 4194304 | tf_op jit(solution)/shard_map/terms/pallas_call | solution.py:187
  67.0 0.0 copy-done.8
  67.0 0.2 fusion.3.level_ref
  67.2 0.0 copy-done
  67.2 25.5 %finish.1 = (f32[2,32,2048]{2,1,0:T(8,128)S(1)}, f32[2,32,2048]{2,1,0:T(8,128)S(1)}, f32[8,128]{1,0:T(8,128)S(1)}) custom-call(s32[2,2]{1,0:T(2,128)S(1)} %copy-done.2, f32[2]{0:T(128)S(1)} %fusion.3.level_ref, f32[2,2048,128]{2,1,0:T(8,128)S(1)} %terms.1.part_ref, bf16[2,32,2048]{2,1,0:T(8,128)(2,1)S(1)} %copy-done.1, f32[3,2,32,2048]{3,2,1,0:T(8,128)S(1)} %copy-done), custom_call_target="tpu_custom_call" | custom-call | tf_op jit(solution)/shard_map/finish/pallas_call | solution.py:402
  92.7 0.5 slice.17
  93.2 0.6 slice_reduce_fusion
  93.8 0.8 copy.21
  94.6 0.8 copy.22
  (11 shorter events, 0.0 us)
Async XLA Ops:
  13.9 1.9 %copy-start.6 = (bf16[8,16,16]{2,1,0:T(8,128)(2,1)S(1)}, bf16[8,16,16]{2,1,0:T(8,128)(2,1)}, u32[]{:S(2)}) copy-start(bf16[8,16,16]{2,1,0:T(8,128)(2,1)} %param.13) | copy-start | bytes 12292
  13.9 2.0 %copy-start.3 = (bf16[2,32,128,128]{3,2,1,0:T(8,128)(2,1)S(1)}, bf16[2,32,128,128]{3,2,1,0:T(8,128)(2,1)}, u32[]{:S(2)}) copy-start(bf16[2,32,128,128]{3,2,1,0:T(8,128)(2,1)} %left_ref.1) | copy-start | bytes 6291460
  13.9 2.0 %copy-start.5 = (s32[32]{0:T(128)S(1)}, s32[32]{0:T(128)}, u32[]{:S(2)}) copy-start(s32[32]{0:T(128)} %op_ref.1) | copy-start | bytes 388
  16.0 1.6 %copy-start.4 = (bf16[2,32,128,128]{3,2,1,0:T(8,128)(2,1)S(1)}, bf16[2,32,128,128]{3,2,1,0:T(8,128)(2,1)}, u32[]{:S(2)}) copy-start(bf16[2,32,128,128]{3,2,1,0:T(8,128)(2,1)} %right_ref.1) | copy-start | bytes 6291460
  17.6 49.4 %copy-start.7 = (f32[16]{0:T(128)S(1)}, f32[16]{0:T(128)}, u32[]{:S(2)}) copy-start(f32[16]{0:T(128)} %param.14) | copy-start | bytes 196
  17.6 49.4 %copy-start.8 = (s32[2]{0:T(128)S(1)}, s32[2]{0:T(128)}, u32[]{:S(2)}) copy-start(s32[2]{0:T(128)} %param.15) | copy-start | bytes 28
  17.6 49.6 %copy-start = (f32[3,2,32,2048]{3,2,1,0:T(8,128)S(1)}, f32[3,2,32,2048]{3,2,1,0:T(8,128)}, u32[]{:S(2)}) copy-start(f32[3,2,32,2048]{3,2,1,0:T(8,128)} %basis_hbm.1) | copy-start | bytes 4718596
  17.6 49.6 %copy-start.1 = (bf16[2,32,2048]{2,1,0:T(8,128)(2,1)S(1)}, bf16[2,32,2048]{2,1,0:T(8,128)(2,1)}, u32[]{:S(2)}) copy-start(bf16[2,32,2048]{2,1,0:T(8,128)(2,1)} %psi_ref.3) | copy-start | bytes 786436
  17.6 49.6 %copy-start.2 = (s32[2,2]{1,0:T(2,128)S(1)}, s32[2,2]{1,0:T(2,128)}, u32[]{:S(2)}) copy-start(s32[2,2]{1,0:T(2,128)} %dims_ref.1) | copy-start | bytes 52

commit v2 on v1

--- a/solution.py
+++ b/solution.py
@@ -10,15 +10,22 @@
 MESH = pl.DeviceIdType.MESH
 
 
-def gather_kernel(n, sectors, psi_ref, out_ref, own_sem, send, recv, fsend, frecv):
+def gather_kernel(n, sectors, flat, psi_ref, out_ref, own_sem, send, recv, fsend, frecv):
     row = lax.axis_index("sector")
     me = lax.axis_index("mpo")
     chips = n // 2
     core, chip = lax.rem(me, 2), lax.div(me, 2)
     sib = chip * 2 + 1 - core
 
+    rows = psi_ref.shape[1]
+
     def at(hop):
         return lax.rem(chip + hop, chips) * 2
+
+    def slot(block, s):
+        if flat:
+            return out_ref.at[s, pl.ds(pl.multiple_of(block * rows, rows), rows)]
+        return out_ref.at[block, s]
 
     barrier = pltpu.get_barrier_semaphore()
     for hop in range(1, chips):
@@ -29,7 +36,7 @@
     def push(src, block, s, to, ssem, rsem):
         return pltpu.make_async_remote_copy(
             src_ref=src,
-            dst_ref=out_ref.at[block, s],
+            dst_ref=slot(block, s),
             send_sem=ssem,
             recv_sem=rsem,
             device_id=(row, to),
@@ -46,18 +53,21 @@
     for s in range(sectors):
         near[s] = push(psi_ref.at[s], me, s, sib, send.at[0, s], recv.at[0, s])
         near[s].start()
-    own = pltpu.make_async_copy(psi_ref, out_ref.at[me], own_sem)
-    own.start()
+    own = [
+        pltpu.make_async_copy(psi_ref.at[s], slot(me, s), own_sem.at[s]) for s in range(sectors)
+    ]
+    for copy in own:
+        copy.start()
     for s in range(sectors):
         for hop in range(1, chips):
             far[hop, s].wait_recv()
             block = at(chips - hop) + core
             relay[hop, s] = push(
-                out_ref.at[block, s], block, s, sib, fsend.at[hop, s], frecv.at[hop, s]
+                slot(block, s), block, s, sib, fsend.at[hop, s], frecv.at[hop, s]
             )
             relay[hop, s].start()
-    own.wait()
-    for s in range(sectors):
+    for s in range(sectors):
+        own[s].wait()
         near[s].wait()
         for hop in range(1, chips):
             far[hop, s].wait_send()
@@ -67,16 +77,21 @@
 def gather(psi, n):
     sectors, rows, width = psi.shape
     chips = n // 2
-    return pl.pallas_call(
-        functools.partial(gather_kernel, n, sectors),
-        out_shape=jax.ShapeDtypeStruct((n, sectors, rows, width), psi.dtype),
+    flat = rows % 16 == 0
+    shape = (sectors, n * rows, width) if flat else (n, sectors, rows, width)
+    out = pl.pallas_call(
+        functools.partial(gather_kernel, n, sectors, flat),
+        out_shape=jax.ShapeDtypeStruct(shape, psi.dtype),
         in_specs=[pl.BlockSpec(memory_space=pl.ANY)],
         out_specs=pl.BlockSpec(memory_space=pl.ANY),
-        scratch_shapes=[pltpu.SemaphoreType.DMA(())]
+        scratch_shapes=[pltpu.SemaphoreType.DMA((sectors,))]
         + [pltpu.SemaphoreType.DMA((chips, sectors))] * 4,
         compiler_params=pltpu.CompilerParams(collective_id=0, has_side_effects=True),
         name="gather",
     )(psi)
+    if flat:
+        return out
+    return jnp.transpose(out, (1, 0, 2, 3)).reshape(sectors, n * rows, width)
 
 
 def terms_kernel(
@@ -86,6 +101,7 @@
     blk = left_ref.shape[2]
     op_count = count.shape[0]
     slots = lists.shape[1]
+    pitch = sums.shape[1] // size_p
 
     for o in range(op_count):
         count[o] = 0
@@ -122,35 +138,38 @@
 
     sums[...] = jnp.zeros_like(sums)
 
-    def pair(i, c):
-        k1, k2 = lists[0, 2 * i], lists[0, 2 * i + 1]
-        used = lists[1, 2 * i + 1]
-        o = lists[2, i]
-        left = jnp.concatenate([left_ref[0, k1], left_ref[0, k2]], axis=0)
-        second = right_ref[0, k2]
-        second = jnp.where(used > 0, second, jnp.zeros_like(second))
-        right = jnp.concatenate([right_ref[0, k1], second], axis=0)
-        step = 2
-        for t in range(size_p // step):
-            cols = pl.ds(t * step * blk, step * blk)
-            v = jnp.dot(left, x_ref[0, :, cols], preferred_element_type=jnp.float32)
-            v = v.astype(jnp.bfloat16)
+    def pairs(i, c):
+        lefts, rights, ops_at = [], [], []
+        for at in (2 * i, 2 * i + 1):
+            k1, k2 = lists[0, 2 * at], lists[0, 2 * at + 1]
+            lefts += [left_ref[0, k1], left_ref[0, k2]]
+            r1, r2 = right_ref[0, k1], right_ref[0, k2]
+            r1 = jnp.where(lists[1, 2 * at] > 0, r1, jnp.zeros_like(r1))
+            r2 = jnp.where(lists[1, 2 * at + 1] > 0, r2, jnp.zeros_like(r2))
+            rights.append(jnp.concatenate([r1, r2], axis=0))
+            ops_at.append(lists[2, at])
+        v = jnp.dot(
+            jnp.concatenate(lefts, axis=0), x_ref[0], preferred_element_type=jnp.float32
+        ).astype(jnp.bfloat16)
+        for j in range(2):
+            w = v[2 * j * blk : 2 * (j + 1) * blk]
             both = [
                 jnp.concatenate(
-                    [v[:blk, u * blk : (u + 1) * blk], v[blk:, u * blk : (u + 1) * blk]], axis=1
+                    [w[:blk, p * blk : (p + 1) * blk], w[blk:, p * blk : (p + 1) * blk]], axis=1
                 )
-                for u in range(step)
+                for p in range(size_p)
             ]
-            both = jnp.concatenate(both, axis=0)
-            start = pl.multiple_of(o * size_p * blk, blk) + t * step * blk
-            rows = pl.ds(pl.multiple_of(start, blk), step * blk)
-            sums[rows, :] = sums[rows, :] + jnp.dot(
-                both, right, preferred_element_type=jnp.float32
-            )
+            m = jnp.dot(
+                jnp.concatenate(both, axis=0), rights[j], preferred_element_type=jnp.float32
+            )
+            for p in range(size_p):
+                rows = pl.ds(p * pitch, blk)
+                sums[ops_at[j], rows, :] = sums[ops_at[j], rows, :] + m[p * blk : (p + 1) * blk]
         return c
 
-    lax.fori_loop(0, total, pair, 0)
-
+    lax.fori_loop(0, lax.div(total + 1, 2), pairs, 0)
+
+    flat = sums.reshape(op_count * size_p * pitch, blk)
     opmat = opmat_ref[...]
     depth = op_count * size_p
 
@@ -158,7 +177,7 @@
         for u in range(4):
             a = i * 8 + u * 2
             y = jnp.concatenate(
-                [sums[pl.ds(a, depth, stride=blk), :], sums[pl.ds(a + 1, depth, stride=blk), :]],
+                [flat[pl.ds(a, depth, stride=pitch), :], flat[pl.ds(a + 1, depth, stride=pitch), :]],
                 axis=1,
             )
             high = y.astype(jnp.bfloat16)
@@ -197,10 +216,10 @@
         ],
         out_specs=pl.BlockSpec((1, blk * size_p, blk), lambda s: (s, 0, 0)),
         scratch_shapes=[
-            pltpu.VMEM((op_count * size_p * blk, blk), jnp.float32),
+            pltpu.VMEM((op_count, size_p * (blk + 8), blk), jnp.float32),
             pltpu.SMEM((op_count,), jnp.int32),
             pltpu.SMEM((op_count,), jnp.int32),
-            pltpu.SMEM((3, terms + op_count + 2), jnp.int32),
+            pltpu.SMEM((3, terms + op_count + 8), jnp.int32),
         ],
         compiler_params=pltpu.CompilerParams(vmem_limit_bytes=44 * 2**20),
         cost_estimate=pl.CostEstimate(
@@ -239,6 +258,7 @@
     basis_ref,
     mine,
     theirs,
+    away,
     landed,
     slots_m,
     slots_s,
@@ -301,10 +321,12 @@
         for s in range(sectors):
             loads[hop, s].wait()
             swaps[hop, s].wait_recv()
-            mine[hop, s] = mine[hop, s] + theirs[hop, s]
-            if hop:
+            if hop == 0:
+                mine[0, s] = mine[0, s] + theirs[0, s]
+            else:
+                away[hop - 1, s] = (mine[hop, s] + theirs[hop, s]).astype(jnp.bfloat16)
                 sends[hop, s] = pltpu.make_async_remote_copy(
-                    src_ref=mine.at[hop, s],
+                    src_ref=away.at[hop - 1, s],
                     dst_ref=landed.at[hop - 1, s],
                     send_sem=send2.at[hop, s],
                     recv_sem=recv2.at[hop, s],
@@ -321,14 +343,13 @@
     for s in range(sectors):
         for hop in range(1, chips):
             sends[hop, s].wait_recv()
+            mine[0, s] = mine[0, s] + landed[hop - 1, s].astype(jnp.float32)
         mask = (row_at < dims_ref[s, 0]) & (col_at < dims_ref[s, 1])
         level = level_ref[s]
         for p in range(size_p):
             cols = slice(p * blk, (p + 1) * blk)
             spots = pl.ds(p, rows, stride=size_p)
             core_p = mine[0, s, spots, :]
-            for hop in range(1, chips):
-                core_p = core_p + landed[hop - 1, s, spots, :]
             x = jnp.where(mask, psi_ref[s, :, cols].astype(jnp.float32), zero)
             h = jnp.where(mask, level * x + core_p, zero)
             hpsi_ref[s, :, cols] = h
@@ -408,7 +429,8 @@
             pltpu.VMEM(basis.shape, jnp.float32),
             pltpu.VMEM((chips, sectors, chunk, blk), jnp.float32),
             pltpu.VMEM((chips, sectors, chunk, blk), jnp.float32),
-            pltpu.VMEM((max(chips - 1, 1), sectors, chunk, blk), jnp.float32),
+            pltpu.VMEM((max(chips - 1, 1), sectors, chunk, blk), jnp.bfloat16),
+            pltpu.VMEM((max(chips - 1, 1), sectors, chunk, blk), jnp.bfloat16),
             pltpu.VMEM((n, 8, blk), jnp.float32),
             pltpu.VMEM((groups, 8, blk), jnp.float32),
             pltpu.VMEM((2, 8, blk), jnp.float32),
@@ -431,7 +453,7 @@
 def body(n, groups, psi, left_env, right_env, term_op, ops, energy, charge, block_dims, basis):
     blk = left_env.shape[-1]
     sectors, rows, width = psi.shape
-    x = jnp.transpose(gather(psi, n), (1, 0, 2, 3)).reshape(sectors, n * rows, width)
+    x = gather(psi, n)
     rows_ok = jnp.arange(blk, dtype=jnp.int32)[None, :, None] < block_dims[:, 0][:, None, None]
     cols_ok = (jnp.arange(width, dtype=jnp.int32) % blk)[None, None, :] < block_dims[:, 1][
         :, None, None

time: 95.3 us -> 78.4 us (0.82)
  Pallas kernels: 87 us -> 69.7 us
  local copies, waits for them, and re-layouts: 6.89 us -> 5.5 us
  other arithmetic: 0.72 us -> 1.94 us
    pallas_call x1, Pallas kernels: 49.4 us -> 35.7 us  [local_terms(): pl.pallas_call(functools.partial(terms_kernel, size_p), out_shape=jax.Sha...]
    pallas_call x1, Pallas kernels: 25.5 us -> 21.9 us  [finish(): pl.pallas_call(functools.partial(finish_kernel, n, groups, cells), out_sh...]
    transpose x1 -> x0, local copies, waits for them, and re-layouts: 1.47 us -> none  [body(): jnp.transpose(gather(psi, n), (1, 0, 2, 3))]
    select_n x1, other arithmetic: 0.38 us -> 1.6 us  [body(): x = jnp.where(rows_ok & cols_ok, x, jnp.zeros_like(x))]
where the time goes in v2:
time: 78.4 us; the launch traced here: 77.9 us
  Pallas kernels  69.7 us (89%)
  local copies, waits for them, and re-layouts  5.5 us (7%)
  other arithmetic  1.94 us (2%)
    pallas_call x1, Pallas kernels, local_terms(): pl.pallas_call(functools.partial(terms_kernel, size_p), out_shape=jax.Sha...  35.7 us
    pallas_call x1, Pallas kernels, finish(): pl.pallas_call(functools.partial(finish_kernel, n, groups, cells), out_sh...  21.9 us
    pallas_call x1, Pallas kernels, gather(): pl.pallas_call(functools.partial(gather_kernel, n, sectors, flat), out_sh...  12.1 us
    unnamed x20, local copies, waits for them, and re-layouts  3.21 us
    select_n x1, other arithmetic, body(): x = jnp.where(rows_ok & cols_ok, x, jnp.zeros_like(x))  1.6 us

profile of v2, /device:TPU:0, one launch (start us, length us, event | category | flops | bytes accessed | tf_op | source)
XLA Modules:
  0.0 77.9 jit_solution(225110678184710212)
XLA Ops:
  0.6 0.0 copy-start.6
  0.6 0.0 copy-start.3
  0.7 0.0 copy-start.5
  0.7 1.1 %slice_reduce_fusion.2 = (s32[2]{0:T(128)S(1)}, s32[2]{0:T(128)S(1)}) fusion(s32[2,2]{1,0:T(2,128)} %dims_ref.1), kind=kLoop, calls=%fused_computation.12 | loop fusion | bytes 32 | tf_op jit(solution)/shard_map/slice | solution.py:457
  1.7 0.1 broadcast_compare_fusion
  1.8 0.1 iota_compare_fusion
  1.9 12.1 %gather.1 = bf16[2,128,2048]{2,1,0:T(8,128)(2,1)} custom-call(bf16[2,32,2048]{2,1,0:T(8,128)(2,1)} %psi_ref.3), custom_call_target="tpu_custom_call" | custom-call | tf_op jit(solution)/shard_map/gather/pallas_call | solution.py:82
  14.0 1.6 %and_select_fusion.x_ref = bf16[2,128,2048]{2,1,0:T(8,128)(2,1)S(1)} fusion(bf16[2,128,2048]{2,1,0:T(8,128)(2,1)} %gather.1, pred[2,2048]{1,0:T(4,128)(4,1)S(1)} %broadcast_compare_fusion, pred[2,128]{1,0:T(4,128)(4,1)S(1)} %iota_compare_fusion), kind=kLoop, calls=%fused_computation | loop fusion | flops 1048576 | bytes 2101504 | tf_op jit(solution)/shard_map/jit(_where)/select_n | solution.py:461
  15.6 0.0 copy-done.6
  15.7 0.1 reshape.80
  15.8 0.0 copy-done.3
  15.8 0.0 copy-done.5
  15.8 0.0 copy-start.4
  15.8 1.6 %copy-done.4 = bf16[2,32,128,128]{3,2,1,0:T(8,128)(2,1)S(1)} copy-done((bf16[2,32,128,128]{3,2,1,0:T(8,128)(2,1)S(1)}, bf16[2,32,128,128]{3,2,1,0:T(8,128)(2,1)}, u32[]{:S(2)}) %copy-start.4) | copy-done | bytes 2097176
  17.4 0.0 copy-start.2
  17.4 35.7 %terms.1.part_ref = f32[2,2048,128]{2,1,0:T(8,128)S(1)} custom-call(s32[32]{0:T(128)S(1)} %copy-done.5, bf16[16,256]{1,0:T(8,128)(2,1)S(1)} %pad_maximum_fusion.opmat_ref, bf16[2,128,2048]{2,1,0:T(8,128)(2,1)S(1)} %and_select_fusion.x_ref, bf16[2,32,128,128]{3,2,1,0:T(8,128)(2,1)S(1)} %copy-done.3, bf16[2,32,128,128]{3,2,1,0:T(8,128)(2,1)S(1)} %copy-done.4), custom_call_target="tpu_custom_call" | custom-call | flops 8589934592 | bytes 4194304 | tf_op jit(solution)/shard_map/terms/pallas_call | solution.py:206
  53.1 0.0 copy-done.7
  53.1 0.2 fusion.3.level_ref
  53.3 0.0 copy-done
  53.3 21.9 %finish.1 = (f32[2,32,2048]{2,1,0:T(8,128)S(1)}, f32[2,32,2048]{2,1,0:T(8,128)S(1)}, f32[8,128]{1,0:T(8,128)S(1)}) custom-call(s32[2,2]{1,0:T(2,128)S(1)} %copy-done.2, f32[2]{0:T(128)S(1)} %fusion.3.level_ref, f32[2,2048,128]{2,1,0:T(8,128)S(1)} %terms.1.part_ref, bf16[2,32,2048]{2,1,0:T(8,128)(2,1)S(1)} %copy-done.1, f32[3,2,32,2048]{3,2,1,0:T(8,128)S(1)} %copy-done), custom_call_target="tpu_custom_call" | custom-call | tf_op jit(solution)/shard_map/finish/pallas_call | solution.py:423
  75.2 0.5 slice.17
  75.7 0.6 slice_reduce_fusion
  76.3 0.8 %copy.18 = f32[2,32,2048]{2,1,0:T(8,128)} copy(f32[2,32,2048]{2,1,0:T(8,128)S(1)} %get-tuple-element.16) | data formatting | bytes 1048576
  77.1 0.8 %copy.19 = f32[2,32,2048]{2,1,0:T(8,128)} copy(f32[2,32,2048]{2,1,0:T(8,128)S(1)} %get-tuple-element.17) | data formatting | bytes 1048576
  (10 shorter events, 0.0 us)
Async XLA Ops:
  0.6 15.0 %copy-start.6 = (bf16[8,16,16]{2,1,0:T(8,128)(2,1)S(1)}, bf16[8,16,16]{2,1,0:T(8,128)(2,1)}, u32[]{:S(2)}) copy-start(bf16[8,16,16]{2,1,0:T(8,128)(2,1)} %param.13) | copy-start | bytes 12292
  0.6 15.1 %copy-start.3 = (bf16[2,32,128,128]{3,2,1,0:T(8,128)(2,1)S(1)}, bf16[2,32,128,128]{3,2,1,0:T(8,128)(2,1)}, u32[]{:S(2)}) copy-start(bf16[2,32,128,128]{3,2,1,0:T(8,128)(2,1)} %left_ref.1) | copy-start | bytes 6291460
  0.7 15.1 %copy-start.5 = (s32[32]{0:T(128)S(1)}, s32[32]{0:T(128)}, u32[]{:S(2)}) copy-start(s32[32]{0:T(128)} %op_ref.1) | copy-start | bytes 388
  15.8 1.6 %copy-start.4 = (bf16[2,32,128,128]{3,2,1,0:T(8,128)(2,1)S(1)}, bf16[2,32,128,128]{3,2,1,0:T(8,128)(2,1)}, u32[]{:S(2)}) copy-start(bf16[2,32,128,128]{3,2,1,0:T(8,128)(2,1)} %right_ref.1) | copy-start | bytes 6291460
  17.4 35.7 %copy-start.7 = (f32[16]{0:T(128)S(1)}, f32[16]{0:T(128)}, u32[]{:S(2)}) copy-start(f32[16]{0:T(128)} %param.14) | copy-start | bytes 196
  17.4 35.7 %copy-start.8 = (s32[2]{0:T(128)S(1)}, s32[2]{0:T(128)}, u32[]{:S(2)}) copy-start(s32[2]{0:T(128)} %param.15) | copy-start | bytes 28
  17.4 35.9 %copy-start = (f32[3,2,32,2048]{3,2,1,0:T(8,128)S(1)}, f32[3,2,32,2048]{3,2,1,0:T(8,128)}, u32[]{:S(2)}) copy-start(f32[3,2,32,2048]{3,2,1,0:T(8,128)} %basis_hbm.1) | copy-start | bytes 4718596
  17.4 35.9 %copy-start.1 = (bf16[2,32,2048]{2,1,0:T(8,128)(2,1)S(1)}, bf16[2,32,2048]{2,1,0:T(8,128)(2,1)}, u32[]{:S(2)}) copy-start(bf16[2,32,2048]{2,1,0:T(8,128)(2,1)} %psi_ref.3) | copy-start | bytes 786436
  17.4 35.9 %copy-start.2 = (s32[2,2]{1,0:T(2,128)S(1)}, s32[2,2]{1,0:T(2,128)}, u32[]{:S(2)}) copy-start(s32[2,2]{1,0:T(2,128)} %dims_ref.1) | copy-start | bytes 52
